TPU v7x, 32 devices: a whole 2x2x4 slice. The times are simulated.
32 devices in a mesh: groups: 2 (over y), span: 2 (over x), tok: 4 (over z), head: 2 (over core).
Axes of the slice: x: 2, y: 2, z: 4, core: 2. Of those that a mesh axis runs over, the one named last changes fastest.
Arguments:
- queries: bfloat16 [16384, 2, 256], P(('groups', 'span', 'tok'), 'head'), parts along dimension 0, may hold values from -6 to 6
- keys: bfloat16 [16384, 2, 256], P(('groups', 'span', 'tok'), 'head'), parts along dimension 0, may hold values from -6 to 6
- values: bfloat16 [16384, 2, 256], P(('groups', 'span', 'tok'), 'head'), parts along dimension 0, may hold values from -6 to 6
- rates: float32 [16384, 2], P(('groups', 'span', 'tok'), 'head'), parts along dimension 0, may hold values from 0.0001 to 0.001
- w_in: bfloat16 [2, 2, 256, 256], P('head'), may hold values from -0.375 to 0.375
- w_out: bfloat16 [2, 256, 256], P('head'), may hold values from -0.375 to 0.375
- gain: float32 [2, 256], P('head'), may hold values from 0.1 to 1.9
- block_doc: int32 [128], P('groups'), parts along dimension 0, may hold values from 0 to 15, never falling along the last dimension, each value on 1 to 8 neighbouring positions
Outputs:
- mixed: bfloat16 [16384, 2, 256], P(('groups', 'span', 'tok'), 'head'), parts along dimension 0
There are 2 independent parts, one for each index of `groups`. A program takes and returns all parts, laid end to end along the dimension named above; an argument that names none is the same for every part. Nothing has to cross between parts.
Inputs may be any that keep to these rules, and one draw needn't show every extreme that they name: block_doc never falls from one block to the next; each document covers 1 to 8 consecutive blocks, one exactly 8.
All inputs are finite; a program needn't handle non-finite values.
Results may differ from a plain program's by a relative error of at most 0.01.
Values may be sent and summed in bfloat16 or wider, within the bound.
A program may use at most 64 MiB of HBM per device.

v0:
```python
import math

import jax
import jax.numpy as jnp
from jax import lax
from jax.sharding import PartitionSpec as P

BLOCK = 128


EPSILON = 1e-06


def from_behind(block, axis, distance):
    devices = range(lax.axis_size(axis))
    route = [(i - distance, i) for i in devices if i - distance in devices]
    return lax.ppermute(block, axis, route)


def rms_scale(inputs):
    return inputs * lax.rsqrt(jnp.mean(inputs * inputs, axis=-1, keepdims=True) + EPSILON)


def silu_slope(pre):
    sigmoid_val = jax.nn.sigmoid(pre)
    return sigmoid_val * (1.0 + pre * (1.0 - sigmoid_val))


def renormalize(updated, row_norm):
    scale = row_norm * lax.rsqrt(jnp.sum(updated * updated, axis=-1, keepdims=True) + EPSILON)
    return (updated * scale).astype(jnp.bfloat16)


def local_gradient(keys_norm, values, rates, w_in, w_out):
    gate_pre = jnp.einsum("thd,hfd->thf", keys_norm, w_in[:, 0], preferred_element_type=jnp.float32)
    up_pre = jnp.einsum("thd,hfd->thf", keys_norm, w_in[:, 1], preferred_element_type=jnp.float32)
    activation = (jax.nn.silu(gate_pre) * up_pre).astype(jnp.bfloat16)
    target = (-(rates[:, :, None] * values.astype(jnp.float32))).astype(jnp.bfloat16)
    act_grad = jnp.einsum("thd,hdf->thf", target, w_out, preferred_element_type=jnp.float32)
    gate_grad = (act_grad * up_pre * silu_slope(gate_pre)).astype(jnp.bfloat16)
    up_grad = (act_grad * jax.nn.silu(gate_pre)).astype(jnp.bfloat16)
    stacked = jnp.stack([gate_grad, up_grad], axis=1)
    grad_in = jnp.einsum("tchf,thd->hcfd", stacked, keys_norm, preferred_element_type=jnp.float32)
    grad_out = jnp.einsum("thd,thf->hdf", target, activation, preferred_element_type=jnp.float32)
    return (grad_in, grad_out)


def attend_blocks(query_norm, keys_norm, values, prior_keys, prior_values, prior_open):
    tokens, heads, width = query_norm.shape
    block_count = tokens // BLOCK
    shape = (block_count, BLOCK, heads, width)
    window_keys = jnp.concatenate([prior_keys.reshape(shape), keys_norm.reshape(shape)], axis=1)
    window_values = jnp.concatenate([prior_values.reshape(shape), values.reshape(shape)], axis=1)
    scores = jnp.einsum(
        "nqhd,nkhd->nhqk",
        query_norm.reshape(shape),
        window_keys,
        preferred_element_type=jnp.float32,
    ) / math.sqrt(width)
    row_pos = lax.broadcasted_iota(jnp.int32, (BLOCK, 2 * BLOCK), 0)
    col_pos = lax.broadcasted_iota(jnp.int32, (BLOCK, 2 * BLOCK), 1)
    inside = col_pos - BLOCK <= row_pos
    visible = jnp.where(col_pos[None] < BLOCK, prior_open[:, None, None], inside[None])
    weights = jnp.where(visible[:, None], jnp.exp(scores), 0.0)
    probabilities = (weights / jnp.sum(weights, axis=-1, keepdims=True)).astype(jnp.bfloat16)
    attended = jnp.einsum(
        "nhqk,nkhd->nqhd", probabilities, window_values, preferred_element_type=jnp.float32
    )
    return attended.reshape(tokens, heads, width)


def body(queries, keys, values, rates, w_in, w_out, gain, block_doc):
    query_norm = rms_scale(queries.astype(jnp.float32)).astype(jnp.bfloat16)
    keys_norm = rms_scale(keys.astype(jnp.float32)).astype(jnp.bfloat16)
    span_pos = lax.axis_index("span")
    span_count = lax.axis_size("span")
    tok_pos = lax.axis_index("tok")
    tok_count = lax.axis_size("tok")
    norm_in = jnp.sqrt(jnp.sum(jnp.square(w_in.astype(jnp.float32)), axis=-1, keepdims=True))
    norm_out = jnp.sqrt(jnp.sum(jnp.square(w_out.astype(jnp.float32)), axis=-1, keepdims=True))
    zeros_in = jnp.zeros(w_in.shape, jnp.float32)
    zeros_out = jnp.zeros(w_out.shape, jnp.float32)
    hidden_rows = w_in.shape[2] // tok_count
    feature_rows = w_out.shape[1] // tok_count

    def shard_of(full_in, full_out):
        return (
            lax.dynamic_slice_in_dim(full_in, tok_pos * hidden_rows, hidden_rows, 2),
            lax.dynamic_slice_in_dim(full_out, tok_pos * feature_rows, feature_rows, 1),
        )

    part_norm_in, part_norm_out = shard_of(norm_in, norm_out)

    def gradient_at(link_step, full_in, full_out):
        return lax.cond(
            span_pos == link_step,
            lambda: local_gradient(keys_norm, values, rates, full_in, full_out),
            lambda: (zeros_in, zeros_out),
        )

    def advance(link_step, state_carry):
        full_in, full_out, own_in, own_out = state_carry
        grad_in, grad_out = gradient_at(link_step, full_in, full_out)
        sum_in, sum_out = (
            lax.psum_scatter(
                grad_in.astype(jnp.bfloat16), "tok", scatter_dimension=2, tiled=True
            ).astype(jnp.float32),
            lax.psum_scatter(
                grad_out.astype(jnp.bfloat16), "tok", scatter_dimension=1, tiled=True
            ).astype(jnp.float32),
        )
        new_in = renormalize(own_in.astype(jnp.float32) - sum_in, part_norm_in)
        new_out = renormalize(own_out.astype(jnp.float32) - sum_out, part_norm_out)
        got_in, got_out = from_behind((new_in, new_out), "span", 1)
        receiver = span_pos == link_step + 1
        own_in = jnp.where(receiver, got_in, own_in)
        own_out = jnp.where(receiver, got_out, own_out)
        full_in, full_out = (
            lax.all_gather(own_in, "tok", axis=2, tiled=True),
            lax.all_gather(own_out, "tok", axis=1, tiled=True),
        )
        return (full_in, full_out, own_in, own_out)

    start_in, start_out = shard_of(w_in, w_out)
    fast_in, fast_out_w, last_in, last_out = lax.fori_loop(
        0, span_count - 1, advance, (w_in, w_out, start_in, start_out)
    )
    gate_pre = jnp.einsum(
        "thd,hfd->thf", query_norm, fast_in[:, 0], preferred_element_type=jnp.float32
    )
    up_pre = jnp.einsum(
        "thd,hfd->thf", query_norm, fast_in[:, 1], preferred_element_type=jnp.float32
    )
    activation = (jax.nn.silu(gate_pre) * up_pre).astype(jnp.bfloat16)
    fast_output = jnp.einsum(
        "thf,hdf->thd", activation, fast_out_w, preferred_element_type=jnp.float32
    )
    ttt = rms_scale(fast_output) * gain[None]
    before_keys, before_values = from_behind(
        (keys_norm[-BLOCK:], values[-BLOCK:]), ("span", "tok"), 1
    )
    prior_keys = jnp.concatenate([before_keys, keys_norm[:-BLOCK]], axis=0)
    prior_values = jnp.concatenate([before_values, values[:-BLOCK]], axis=0)
    block_count = queries.shape[0] // BLOCK
    device_index = span_pos * tok_count + tok_pos
    padded_docs = jnp.concatenate([jnp.full((1,), -1, jnp.int32), block_doc])
    block_start = device_index * block_count
    prior_docs = lax.dynamic_slice_in_dim(padded_docs, block_start, block_count)
    own_docs = lax.dynamic_slice_in_dim(padded_docs, block_start + 1, block_count)
    prior_open = prior_docs == own_docs
    attended = attend_blocks(query_norm, keys_norm, values, prior_keys, prior_values, prior_open)
    return (attended + ttt).astype(jnp.bfloat16)


def solution(mesh):
    placed = (
        P(("groups", "span", "tok"), "head", None),
        P(("groups", "span", "tok"), "head", None),
        P(("groups", "span", "tok"), "head", None),
        P(("groups", "span", "tok"), "head"),
        P("head", None, None, None),
        P("head", None, None),
        P("head", None),
        P("groups"),
    )
    return jax.shard_map(
        body,
        mesh=mesh,
        in_specs=placed,
        out_specs=P(("groups", "span", "tok"), "head", None),
        check_vma=False,
    )
```

profile of v0, /device:TPU:0, one launch (start us, length us, event | category | flops | bytes accessed | tf_op | source)
XLA Modules:
  0.0 98.3 jit_solution(1689548513804843051)
XLA Ops:
  6.5 0.0 reduce-scatter.3.cloned.1.call-start
  6.6 1.3 %fusion.28 = f32[1024]{0:T(1024)S(1)} fusion(bf16[1024,1,256]{2,0,1:T(8,128)(2,1)} %param.11), kind=kLoop, calls=%fused_computation.43 | loop fusion | flops 785408 | bytes 528384 | tf_op jit(solution)/shard_map/reduce_sum | solution.py:21
  7.9 1.2 %fusion.29 = bf16[1024,1,256]{2,0,1:T(8,128)(2,1)S(1)} fusion(bf16[1024,1,256]{2,0,1:T(8,128)(2,1)} %param.11, f32[1024]{0:T(1024)S(1)} %add_rsqrt_fusion.1), kind=kLoop, calls=%fused_computation.44 | loop fusion | flops 786432 | bytes 1052672 | tf_op jit(solution)/shard_map/convert_element_type | solution.py:74
  9.2 2.6 %conditional.1 = (bf16[1,2,256,256]{3,2,1,0:T(8,128)(2,1)S(1)}, bf16[1,256,256]{2,1,0:T(8,128)(2,1)S(1)}) conditional(s32[]{:T(128)} %convert_element_type.85, () %tuple.15, (f32[1024,1]{0,1:T(1,128)S(1)}, bf16[1024,1,256]{2,0,1:T(8,128)(2,1)S(1)}, bf16[1,256,256]{2,1,0:T(8,128)(2,1)S(1)}, bf16[1,2,256,256]{3,2,1,0:T(8,128)(2,1)S(1)}, ...), branch_computations={%region_3.0_spmd, %region_4.5_spmd} | conditional | flops 812908544 | bytes 11804688 | solution.py:95
  9.2 0.3 convolution_bitcast_fusion
  9.6 0.3 convolution_bitcast_fusion.1
  9.9 0.7 fusion.10
  10.6 0.5 convolution_bitcast_fusion.3
  11.1 0.6 convolution_bitcast_fusion.4
  11.8 0.0 copy-start.2
  11.8 0.6 copy-done.5
  12.4 0.0 reduce-scatter.3.cloned.1.call-update
  12.5 0.0 reduce-scatter.5.cloned.1.call-start
  12.5 4.9 %collective-permute-start.1 = (bf16[128,1,256]{2,0,1:T(8,128)(2,1)S(1)}, bf16[128,1,256]{2,0,1:T(8,128)(2,1)S(1)}, u32[]{:S(2)}, u32[]{:S(2)}) collective-permute-start(bf16[128,1,256]{2,0,1:T(8,128)(2,1)S(1)} %slice.30), channel_id=1, source_target_pairs={{0,2},{2,4},{4,6},{6,8},{8,10},{10,12},{12,14},{1,3},{3,5},{5,7},{... | collective-permute-start | bytes 196616 | tf_op jit(solution)/shard_map/ppermute | solution.py:17
  17.5 3.5 %collective-permute-start = (bf16[128,1,256]{2,0,1:T(8,128)(2,1)S(1)}, bf16[128,1,256]{2,0,1:T(8,128)(2,1)S(1)}, u32[]{:S(2)}, u32[]{:S(2)}) collective-permute-start(bf16[128,1,256]{2,0,1:T(8,128)(2,1)S(1)} %slice.24), channel_id=1, source_target_pairs={{0,2},{2,4},{4,6},{6,8},{8,10},{10,12},{12,14},{1,3},{3,5},{5,7},{... | collective-permute-start | bytes 196616 | tf_op jit(solution)/shard_map/ppermute | solution.py:17
  21.0 0.0 reduce-scatter.5.cloned.1.call-update
  21.0 0.1 multiply_reduce_fusion.1
  21.2 0.0 copy-start
  21.2 0.1 multiply_reduce_fusion.2
  21.4 0.0 copy-start.10
  21.4 0.8 copy-done
  22.2 0.2 fusion.26
  22.4 0.2 fusion.27
  22.7 0.1 pad_add_fusion
  22.8 0.1 dynamic-slice_compare_fusion
  22.9 0.0 collective-permute-done.1
  22.9 1.5 %fusion.23 = f32[8,128,256]{2,1,0:T(8,128)} fusion(bf16[8,128,256]{2,1,0:T(8,128)(2,1)S(1)} %bitcast.130, bf16[8,128,1,256]{3,1,0,2:T(8,128)(2,1)S(1)} %bitcast.129, bf16[8,128,1,256]{3,1,0,2:T(8,128)(2,1)S(1)} %bitcast.133, pred[128,256]{1,0:T(8,128)(4,1)S(1)} %get-tuple-element.71, pred[128,256]{1,0:T(8,128)(4,1)S(1)} %get-tuple-element.72, ...), kind=kOutput, calls=%fused_computation.34 | convolution fusion | flops 137101312 | bytes 2686984 | tf_op jit(solution)/shard_map/nqhd,nkhd->nhqk/dot_general | solution.py:54
  24.4 0.0 collective-permute-done
  24.5 1.0 %copy-done.4 = bf16[1024,1,256]{2,0,1:T(8,128)(2,1)S(1)} copy-done((bf16[1024,1,256]{2,0,1:T(8,128)(2,1)S(1)}, bf16[1024,1,256]{2,0,1:T(8,128)(2,1)}, u32[]{:S(2)}) %copy-start.4) | copy-done | bytes 524312
  25.5 1.9 %fusion.32 = f32[8,256,128]{1,2,0:T(8,128)S(1)} fusion(bf16[8,128,1,256]{3,1,0,2:T(8,128)(2,1)S(1)} %bitcast.132, bf16[8,128,1,256]{3,1,0,2:T(8,128)(2,1)S(1)} %bitcast.134, f32[8,128,256]{2,1,0:T(8,128)} %fusion.23), kind=kOutput, calls=%fused_computation.49 | convolution fusion | flops 136840448 | bytes 3145728 | tf_op jit(solution)/shard_map/nhqk,nkhd->nqhd/dot_general | solution.py:66
  27.4 0.3 copy.19
  27.7 5.8 %reduce-scatter.3.cloned.1.call-done = bf16[1,64,256]{2,1,0:T(8,128)(2,1)} async-done(((bf16[1,256,256]{2,1,0:T(8,128)(2,1)}), bf16[1,64,256]{2,1,0:T(8,128)(2,1)}) %reduce-scatter.3.cloned.1.call-update) | async-done | bytes 32784 | tf_op jit(solution)/shard_map/while/body/eval_jaxpr/reduce_scatter | solution.py:108
  33.6 0.9 multiply_reduce_fusion.4
  34.5 0.1 rsqrt_multiply_fusion
  34.5 0.8 multiply_convert_fusion.4
  35.4 3.3 %collective-permute-start.2 = (bf16[1,64,256]{2,1,0:T(8,128)(2,1)S(1)}, bf16[1,64,256]{2,1,0:T(8,128)(2,1)S(1)}, u32[]{:S(2)}, u32[]{:S(2)}) collective-permute-start(bf16[1,64,256]{2,1,0:T(8,128)(2,1)S(1)} %multiply_convert_fusion.4), channel_id=1, source_target_pairs={{0,8},{1,9},{2,10},{3,11},{4,12},{5,13},{6,14},{7,15},{16,24},{17,... | collective-permute-start | bytes 98312 | tf_op jit(solution)/shard_map/while/body/eval_jaxpr/ppermute | solution.py:17
  38.7 14.9 %reduce-scatter.5.cloned.1.call-done = bf16[1,2,64,256]{3,2,1,0:T(8,128)(2,1)} async-done(((bf16[1,2,256,256]{3,2,1,0:T(8,128)(2,1)}), bf16[1,2,64,256]{3,2,1,0:T(8,128)(2,1)}) %reduce-scatter.5.cloned.1.call-update) | async-done | bytes 65552 | tf_op jit(solution)/shard_map/while/body/eval_jaxpr/reduce_scatter | solution.py:105
  53.6 0.9 multiply_reduce_fusion.3
  54.6 0.1 fusion.44
  54.6 0.9 multiply_convert_fusion.3
  55.6 3.5 %collective-permute-start.3 = (bf16[1,2,64,256]{3,2,1,0:T(8,128)(2,1)S(1)}, bf16[1,2,64,256]{3,2,1,0:T(8,128)(2,1)S(1)}, u32[]{:S(2)}, u32[]{:S(2)}) collective-permute-start(bf16[1,2,64,256]{3,2,1,0:T(8,128)(2,1)S(1)} %multiply_convert_fusion.3), channel_id=1, source_target_pairs={{0,8},{1,9},{2,10},{3,11},{4,12},{5,13},{6,14},{7,15},{16,24},{17,... | collective-permute-start | bytes 196616 | tf_op jit(solution)/shard_map/while/body/eval_jaxpr/ppermute | solution.py:17
  59.1 0.0 collective-permute-done.2
  59.1 13.5 %all_gather.8 = bf16[1,256,256]{2,1,0:T(8,128)(2,1)S(1)} all-gather(bf16[1,64,256]{2,1,0:T(8,128)(2,1)S(1)} %broadcast_select_fusion.1), channel_id=1, replica_groups=mesh['groups'=2,'span'=2,'tok'=4,'head'=2] {'tok'}, dimensions={1}, use_global_device_ids=true | all-gather | bytes 163840 | tf_op jit(solution)/shard_map/while/body/eval_jaxpr/all_gather | solution.py:120
  72.6 14.4 %all_gather.9 = bf16[1,2,256,256]{3,2,1,0:T(8,128)(2,1)S(1)} all-gather(bf16[1,2,64,256]{3,2,1,0:T(8,128)(2,1)S(1)} %broadcast_select_fusion), channel_id=1, replica_groups=mesh['groups'=2,'span'=2,'tok'=4,'head'=2] {'tok'}, dimensions={2}, use_global_device_ids=true | all-gather | bytes 327680 | tf_op jit(solution)/shard_map/while/body/eval_jaxpr/all_gather | solution.py:119
  87.0 1.3 %convolution_bitcast_fusion.7 = f32[1024,1,256]{0,2,1:T(8,128)} fusion(bf16[1024,1,256]{2,0,1:T(8,128)(2,1)S(1)} %fusion.27, bf16[1,2,256,256]{3,2,1,0:T(8,128)(2,1)S(1)} %all_gather.9), kind=kOutput, calls=%fused_computation.31 | convolution fusion | flops 134217728 | bytes 1703936 | tf_op jit(solution)/shard_map/thd,hfd->thf/dot_general | solution.py:128
  88.4 1.9 %multiply_reduce_fusion = (f32[1024]{0:T(1024)S(1)}, f32[1,256,1024]{2,1,0:T(8,128)S(1)}) fusion(f32[1024,1,256]{0,2,1:T(8,128)} %convolution_bitcast_fusion.7, bf16[1024,1,256]{2,0,1:T(8,128)(2,1)S(1)} %fusion.27, bf16[1,2,256,256]{3,2,1,0:T(8,128)(2,1)S(1)} %all_gather.9, bf16[1,256,256]{2,1,0:T(8,128)(2,1)S(1)} %all_gather.8), kind=kOutput, calls=%fused_computation.54 | convolution fusion | flops 270531584 | bytes 2887680 | tf_op jit(solution)/shard_map/thf,hdf->thd/dot_general | solution.py:135
  90.3 0.2 fusion.35
  90.5 1.0 %copy.20 = bf16[1024,1,256]{2,0,1:T(8,128)(2,1)} copy(bf16[1024,1,256]{0,2,1:T(8,128)(2,1)S(1)} %fusion.35) | data formatting | bytes 1048576 | tf_op jit(solution)/shard_map/convert_element_type | solution.py:152
  (31 shorter events, 0.3 us)
Async XLA Ops:
  6.5 2.7 %copy-start.3 = (bf16[1024,1,256]{2,0,1:T(8,128)(2,1)S(1)}, bf16[1024,1,256]{2,0,1:T(8,128)(2,1)}, u32[]{:S(2)}) copy-start(bf16[1024,1,256]{2,0,1:T(8,128)(2,1)} %param.12) | copy-start | bytes 1572868
  6.5 2.7 %copy-start.9 = (f32[1024,1]{0,1:T(1,128)S(1)}, f32[1024,1]{0,1:T(1,128)}, u32[]{:S(2)}) copy-start(f32[1024,1]{0,1:T(1,128)} %param.13) | copy-start | bytes 12292
  6.5 2.7 %copy-start.1 = (bf16[1,2,256,256]{3,2,1,0:T(8,128)(2,1)S(1)}, bf16[1,2,256,256]{3,2,1,0:T(8,128)(2,1)}, u32[]{:S(2)}) copy-start(bf16[1,2,256,256]{3,2,1,0:T(8,128)(2,1)} %param.14) | copy-start | bytes 786436
  6.5 2.7 %copy-start.6 = (bf16[1,256,256]{2,1,0:T(8,128)(2,1)S(1)}, bf16[1,256,256]{2,1,0:T(8,128)(2,1)}, u32[]{:S(2)}) copy-start(bf16[1,256,256]{2,1,0:T(8,128)(2,1)} %param.15) | copy-start | bytes 393220
  6.5 27.0 %reduce-scatter.3.cloned.1.call-start = ((), (), s32[]{:S(2)}) async-start(), calls=%async_computation.2 | async-start | bytes 163840 | tf_op jit(solution)/shard_map/while/body/eval_jaxpr/reduce_scatter | solution.py:108
  11.8 0.6 copy-start.5
  11.8 9.2 %copy-start.2 = (bf16[1,2,256,256]{3,2,1,0:T(8,128)(2,1)}, bf16[1,2,256,256]{3,2,1,0:T(8,128)(2,1)S(1)}, u32[]{:S(2)}) copy-start(bf16[1,2,256,256]{3,2,1,0:T(8,128)(2,1)S(1)} %get-tuple-element.45) | copy-start | bytes 786436
  12.5 41.1 %reduce-scatter.5.cloned.1.call-start = ((), (), s32[]{:S(2)}) async-start(), calls=%async_computation.3 | async-start | bytes 327680 | tf_op jit(solution)/shard_map/while/body/eval_jaxpr/reduce_scatter | solution.py:105
  12.5 10.3 %collective-permute-start.1 = (bf16[128,1,256]{2,0,1:T(8,128)(2,1)S(1)}, bf16[128,1,256]{2,0,1:T(8,128)(2,1)S(1)}, u32[]{:S(2)}, u32[]{:S(2)}) collective-permute-start(bf16[128,1,256]{2,0,1:T(8,128)(2,1)S(1)} %slice.30), channel_id=1, source_target_pairs={{0,2},{2,4},{4,6},{6,8},{8,10},{10,12},{12,14},{1,3},{3,5},{5,7},{... | collective-permute-start | bytes 196616 | tf_op jit(solution)/shard_map/ppermute | solution.py:17
  17.5 6.9 %collective-permute-start = (bf16[128,1,256]{2,0,1:T(8,128)(2,1)S(1)}, bf16[128,1,256]{2,0,1:T(8,128)(2,1)S(1)}, u32[]{:S(2)}, u32[]{:S(2)}) collective-permute-start(bf16[128,1,256]{2,0,1:T(8,128)(2,1)S(1)} %slice.24), channel_id=1, source_target_pairs={{0,2},{2,4},{4,6},{6,8},{8,10},{10,12},{12,14},{1,3},{3,5},{5,7},{... | collective-permute-start | bytes 196616 | tf_op jit(solution)/shard_map/ppermute | solution.py:17
  21.2 1.0 %copy-start = (bf16[1024,1,256]{2,0,1:T(8,128)(2,1)S(1)}, bf16[1024,1,256]{2,0,1:T(8,128)(2,1)}, u32[]{:S(2)}) copy-start(bf16[1024,1,256]{2,0,1:T(8,128)(2,1)} %param.10) | copy-start | bytes 1572868
  21.4 1.3 %copy-start.10 = (s32[64]{0:T(128)S(1)}, s32[64]{0:T(128)}, u32[]{:S(2)}) copy-start(s32[64]{0:T(128)} %param.17) | copy-start | bytes 772
  24.4 1.0 %copy-start.4 = (bf16[1024,1,256]{2,0,1:T(8,128)(2,1)S(1)}, bf16[1024,1,256]{2,0,1:T(8,128)(2,1)}, u32[]{:S(2)}) copy-start(bf16[1024,1,256]{2,0,1:T(8,128)(2,1)} %param.12) | copy-start | bytes 1572868
  27.4 6.2 %copy-start.7 = (bf16[1,256,256]{2,1,0:T(8,128)(2,1)S(1)}, bf16[1,256,256]{2,1,0:T(8,128)(2,1)}, u32[]{:S(2)}) copy-start(bf16[1,256,256]{2,1,0:T(8,128)(2,1)} %param.15) | copy-start | bytes 393220
  35.4 23.7 %collective-permute-start.2 = (bf16[1,64,256]{2,1,0:T(8,128)(2,1)S(1)}, bf16[1,64,256]{2,1,0:T(8,128)(2,1)S(1)}, u32[]{:S(2)}, u32[]{:S(2)}) collective-permute-start(bf16[1,64,256]{2,1,0:T(8,128)(2,1)S(1)} %multiply_convert_fusion.4), channel_id=1, source_target_pairs={{0,8},{1,9},{2,10},{3,11},{4,12},{5,13},{6,14},{7,15},{16,24},{17,... | collective-permute-start | bytes 98312 | tf_op jit(solution)/shard_map/while/body/eval_jaxpr/ppermute | solution.py:17
  55.6 17.1 %collective-permute-start.3 = (bf16[1,2,64,256]{3,2,1,0:T(8,128)(2,1)S(1)}, bf16[1,2,64,256]{3,2,1,0:T(8,128)(2,1)S(1)}, u32[]{:S(2)}, u32[]{:S(2)}) collective-permute-start(bf16[1,2,64,256]{3,2,1,0:T(8,128)(2,1)S(1)} %multiply_convert_fusion.3), channel_id=1, source_target_pairs={{0,8},{1,9},{2,10},{3,11},{4,12},{5,13},{6,14},{7,15},{16,24},{17,... | collective-permute-start | bytes 196616 | tf_op jit(solution)/shard_map/while/body/eval_jaxpr/ppermute | solution.py:17
  88.4 1.9 %copy-start.8 = (f32[1,256]{1,0:T(1,128)S(1)}, f32[1,256]{1,0:T(1,128)}, u32[]{:S(2)}) copy-start(f32[1,256]{1,0:T(1,128)} %param.16) | copy-start | bytes 3076
Sparse Core Ops, SparseCore 0:
  12.6 20.9 reduce-scatter.2
  35.9 17.6 reduce-scatter.4
where the time goes:
time: 98.9 us; the launch traced here: 98.3 us
  blocking collectives  27.9 us (28%)
  waiting for transfers between devices  20.7 us (21%)
  starting transfers between devices  15.3 us (15%)
  between operations  13.8 us (14%)
  matrix products  9.19 us (9%)
  other arithmetic  7.46 us (8%)
  local copies, waits for them, and re-layouts  3.87 us (4%)
    ppermute x4, starting transfers between devices, from_behind(): return lax.ppermute(block, axis, route)  15.2 us
    reduce_scatter x1, waiting for transfers between devices, advance(): lax.psum_scatter(grad_in.astype(jnp.bfloat16), 'tok', scatter_dimension=2...  14.9 us
    all_gather x1, blocking collectives, advance(): lax.all_gather(own_in, 'tok', axis=2, tiled=True)  14.4 us
    all_gather x1, blocking collectives, advance(): lax.all_gather(own_out, 'tok', axis=1, tiled=True)  13.5 us
    reduce_scatter x1, waiting for transfers between devices, advance(): lax.psum_scatter(grad_out.astype(jnp.bfloat16), 'tok', scatter_dimension=...  5.84 us
    unnamed x22, local copies, waits for them, and re-layouts  2.46 us
  transfers between devices with their start and end apart: 6, of which 2 were waited for; matrix products, arithmetic and copies ran while one was open for 9% of the time, Pallas kernels for 0%

commit v1 on v0

v1 whole, which is shorter than its diff:
```python
import functools

import jax
import jax.numpy as jnp
from jax import lax
from jax.experimental import pallas as pl
from jax.experimental.pallas import tpu as pltpu
from jax.sharding import PartitionSpec as P

BLOCK = 128
TILE = 256
EPSILON = 1e-06
MESH = pl.DeviceIdType.MESH
F32 = jnp.float32
BF16 = jnp.bfloat16


def dot_nt(a, b):
    return lax.dot_general(a, b, (((1,), (1,)), ((), ())), preferred_element_type=F32)


def dot_nn(a, b):
    return lax.dot_general(a, b, (((1,), (0,)), ((), ())), preferred_element_type=F32)


def rms_rows(x):
    return x * lax.rsqrt(jnp.mean(x * x, axis=-1, keepdims=True) + EPSILON)


def sigmoid(x):
    return 0.5 * jnp.tanh(0.5 * x) + 0.5


def kernel(
    spans,
    toks,
    q_ref,
    k_ref,
    v_ref,
    rates_ref,
    w_in_ref,
    w_out_ref,
    gain_ref,
    doc_ref,
    out_ref,
    q_raw,
    k_raw,
    v_ext,
    qn,
    kn,
    rates,
    gain,
    doc,
    cur,
    start_rows,
    gate_t,
    up_t,
    act_t,
    grads,
    parts,
    fresh,
    gate_buf,
    act_buf,
    attended,
    out_buf,
    local_sem,
    out_sem,
    halo_send,
    halo_recv,
    part_send,
    part_recv,
    fresh_send,
    fresh_recv,
):
    tokens, width = q_ref.shape
    hidden = cur.shape[1]
    rows = hidden // toks
    blocks = tokens // BLOCK
    tiles = tokens // TILE
    span = lax.axis_index("span")
    tok = lax.axis_index("tok")
    place = span * toks + tok
    own = pl.ds(pl.multiple_of(tok * rows, rows), rows)

    def at(s, t):
        return {"span": s, "tok": t}

    barrier = pltpu.get_barrier_semaphore()
    for k in range(1, toks):
        pl.semaphore_signal(
            barrier, inc=1, device_id=at(span, lax.rem(tok + k, toks)), device_id_type=MESH
        )

    @pl.when(span < spans - 1)
    def _():
        for k in range(toks):
            pl.semaphore_signal(barrier, inc=1, device_id=at(span + 1, k), device_id_type=MESH)

    @pl.when(span > 0)
    def _():
        for k in range(toks):
            pl.semaphore_signal(barrier, inc=1, device_id=at(span - 1, k), device_id_type=MESH)

    k_load = pltpu.make_async_copy(k_ref, k_raw.at[pl.ds(BLOCK, tokens)], local_sem.at[0])
    v_load = pltpu.make_async_copy(v_ref, v_ext.at[pl.ds(BLOCK, tokens)], local_sem.at[1])
    q_load = pltpu.make_async_copy(q_ref, q_raw, local_sem.at[2])
    rates_load = pltpu.make_async_copy(rates_ref, rates, local_sem.at[3])
    gain_load = pltpu.make_async_copy(gain_ref, gain, local_sem.at[4])
    doc_load = pltpu.make_async_copy(doc_ref, doc, local_sem.at[5])
    in_load = pltpu.make_async_copy(w_in_ref, cur.at[pl.ds(0, 2)], local_sem.at[6])
    w_load = pltpu.make_async_copy(w_out_ref, cur.at[2], local_sem.at[7])
    start_in_load = pltpu.make_async_copy(
        w_in_ref.at[:, own], start_rows.at[pl.ds(0, 2)], local_sem.at[8]
    )
    start_out_load = pltpu.make_async_copy(w_out_ref.at[own], start_rows.at[2], local_sem.at[9])
    k_load.start()

    @pl.when(span == 0)
    def _():
        in_load.start()
        w_load.start()

    v_load.start()
    rates_load.start()
    q_load.start()
    doc_load.start()
    gain_load.start()

    @pl.when(span < spans - 1)
    def _():
        start_in_load.start()
        start_out_load.start()

    sides = 1 if spans == 2 else jnp.minimum(span, 1) + jnp.minimum(spans - 1 - span, 1)
    pl.semaphore_wait(barrier, toks - 1 + toks * sides)

    later = lax.rem(place + 1, spans * toks)
    later_at = at(later // toks, lax.rem(later, toks))
    last_rows = pl.ds(tokens - BLOCK, BLOCK)
    halo_k = pltpu.make_async_remote_copy(
        k_ref.at[last_rows],
        k_raw.at[pl.ds(0, BLOCK)],
        halo_send.at[0],
        halo_recv.at[0],
        device_id=later_at,
        device_id_type=MESH,
    )
    halo_v = pltpu.make_async_remote_copy(
        v_ref.at[last_rows],
        v_ext.at[pl.ds(0, BLOCK)],
        halo_send.at[1],
        halo_recv.at[1],
        device_id=later_at,
        device_id_type=MESH,
    )

    @pl.when(place < spans * toks - 1)
    def _():
        halo_k.start()
        halo_v.start()

    def part_copy(c, k):
        target = lax.rem(tok + k, toks)
        return pltpu.make_async_remote_copy(
            grads.at[c, pl.ds(pl.multiple_of(target * rows, rows), rows)],
            parts.at[c, k - 1],
            part_send.at[c, k - 1],
            part_recv.at[c, k - 1],
            device_id=at(span, target),
            device_id_type=MESH,
        )

    def fresh_copy(c, k):
        return pltpu.make_async_remote_copy(
            fresh.at[c],
            cur.at[c, own],
            fresh_send.at[c, k],
            fresh_recv.at[c, k],
            device_id=at(lax.rem(span + 1, spans), lax.rem(tok + k, toks)),
            device_id_type=MESH,
        )

    def norm_keys():
        k_load.wait()
        for i in range(tiles):
            piece = pl.ds(BLOCK + i * TILE, TILE)
            kn[piece] = rms_rows(k_raw[piece].astype(F32)).astype(BF16)

    def send_gradient():
        w_out_t = cur[2].astype(F32).T.astype(BF16)
        for i in range(tiles):
            piece = pl.ds(BLOCK + i * TILE, TILE)
            lanes = pl.ds(i * TILE, TILE)
            keys = kn[piece]
            gate = dot_nt(cur[0], keys)
            up = dot_nt(cur[1], keys)
            step = -rates[:, lanes]
            act_grad = dot_nt(w_out_t, v_ext[piece]) * step
            s = sigmoid(gate)
            silu = gate * s
            act_t[:, lanes] = (silu * up * step).astype(BF16)
            gate_t[:, lanes] = (act_grad * up * (s + silu * (1.0 - s))).astype(BF16)
            up_t[:, lanes] = (act_grad * silu).astype(BF16)
        keys = kn[pl.ds(BLOCK, tokens)]
        grads[0] = dot_nn(gate_t[...], keys).astype(BF16)
        for k in range(1, toks):
            part_copy(0, k).start()
        grads[1] = dot_nn(up_t[...], keys).astype(BF16)
        for k in range(1, toks):
            part_copy(1, k).start()
        grads[2] = dot_nn(act_t[...], v_ext[pl.ds(BLOCK, tokens)]).T.astype(BF16)
        for k in range(1, toks):
            part_copy(2, k).start()

    def pass_on(c):
        total = grads[c, own].astype(F32)
        for k in range(1, toks):
            part_copy(c, k).wait_recv()
            total += parts[c, k - 1].astype(F32)
        first = start_rows[c].astype(F32)
        updated = cur[c, own].astype(F32) - total
        scale = jnp.sqrt(jnp.sum(first * first, axis=-1, keepdims=True)) * lax.rsqrt(
            jnp.sum(updated * updated, axis=-1, keepdims=True) + EPSILON
        )
        fresh[c] = (updated * scale).astype(BF16)
        for k in range(toks):
            fresh_copy(c, k).start()

    def sent():
        for c in range(3):
            for k in range(1, toks):
                part_copy(c, k).wait_send()
            for k in range(toks):
                fresh_copy(c, k).wait_send()

    def norm_queries():
        q_load.wait()
        for i in range(tiles):
            piece = pl.ds(i * TILE, TILE)
            qn[piece] = rms_rows(q_raw[piece].astype(F32)).astype(BF16)

    def attend():
        doc_load.wait()
        row_pos = lax.broadcasted_iota(jnp.int32, (BLOCK, BLOCK), 0)
        col_pos = lax.broadcasted_iota(jnp.int32, (BLOCK, BLOCK), 1)
        inside = col_pos <= row_pos

        def one(b):
            block = place * blocks + b
            before = doc[jnp.maximum(block - 1, 0)]
            same = jnp.where(before == doc[block], 1.0, 0.0).astype(F32)
            same = jnp.where(block > 0, same, 0.0)
            window = pl.ds(b * BLOCK, 2 * BLOCK)
            score = dot_nt(qn[pl.ds(b * BLOCK, BLOCK)], kn[window]) * (width**-0.5)
            weight = jnp.exp(score)
            prior = weight[:, :BLOCK] * same
            here = jnp.where(inside, weight[:, BLOCK:], 0.0)
            both = jnp.concatenate([prior, here], axis=1)
            total = jnp.sum(both, axis=-1, keepdims=True)
            mixed = dot_nn(both.astype(BF16), v_ext[window])
            attended[pl.ds(b * BLOCK, BLOCK)] = mixed / total

        for b in range(1, blocks):
            one(b)

        @pl.when(place > 0)
        def _():
            halo_k.wait_recv()
            halo_v.wait_recv()

        @pl.when(place == 0)
        def _():
            k_raw[pl.ds(0, BLOCK)] = jnp.zeros((BLOCK, width), BF16)
            v_ext[pl.ds(0, BLOCK)] = jnp.zeros((BLOCK, width), BF16)

        kn[pl.ds(0, BLOCK)] = rms_rows(k_raw[pl.ds(0, BLOCK)].astype(F32)).astype(BF16)
        one(0)

    def out_copy(i):
        piece = pl.ds(i * TILE, TILE)
        return pltpu.make_async_copy(out_buf.at[piece], out_ref.at[piece], out_sem.at[i])

    def apply_fast(ready):
        ready(0)
        for i in range(tiles):
            piece = pl.ds(i * TILE, TILE)
            gate_buf[piece] = dot_nt(qn[piece], cur[0])
        ready(1)
        for i in range(tiles):
            piece = pl.ds(i * TILE, TILE)
            gate = gate_buf[piece]
            up = dot_nt(qn[piece], cur[1])
            act_buf[piece] = (gate * sigmoid(gate) * up).astype(BF16)
        ready(2)
        gain_load.wait()
        for i in range(tiles):
            piece = pl.ds(i * TILE, TILE)
            fast = dot_nt(act_buf[piece], cur[2])
            out_buf[piece] = (attended[piece] + rms_rows(fast) * gain[...]).astype(BF16)
            out_copy(i).start()

    def arrived(c):
        for k in range(toks):
            fresh_copy(c, k).wait_recv()

    @pl.when(span == 0)
    def _():
        norm_keys()
        in_load.wait()
        w_load.wait()
        v_load.wait()
        rates_load.wait()
        start_in_load.wait()
        start_out_load.wait()
        send_gradient()
        norm_queries()
        attend()
        pass_on(0)
        pass_on(1)
        pass_on(2)
        apply_fast(lambda c: None)
        sent()

    @pl.when(span > 0)
    def _():
        norm_keys()
        norm_queries()
        v_load.wait()
        rates_load.wait()
        attend()
        if spans > 2:

            @pl.when(span < spans - 1)
            def _():
                start_in_load.wait()
                start_out_load.wait()
                for c in range(3):
                    arrived(c)
                send_gradient()
                for c in range(3):
                    pass_on(c)
                apply_fast(lambda c: None)
                sent()

            @pl.when(span == spans - 1)
            def _():
                apply_fast(arrived)

        else:
            apply_fast(arrived)

    for i in range(tiles):
        out_copy(i).wait()

    @pl.when(place < spans * toks - 1)
    def _():
        halo_k.wait_send()
        halo_v.wait_send()


def body(spans, toks, queries, keys, values, rates, w_in, w_out, gain, block_doc):
    tokens, _, width = queries.shape
    hidden = w_in.shape[2]
    rows = hidden // toks
    tiles = tokens // TILE
    anywhere = pl.BlockSpec(memory_space=pltpu.HBM)
    dma = pltpu.SemaphoreType.DMA
    out = pl.pallas_call(
        functools.partial(kernel, spans, toks),
        out_shape=jax.ShapeDtypeStruct((tokens, width), BF16),
        in_specs=[anywhere] * 8,
        out_specs=anywhere,
        scratch_shapes=[
            pltpu.VMEM((tokens, width), BF16),
            pltpu.VMEM((tokens + BLOCK, width), BF16),
            pltpu.VMEM((tokens + BLOCK, width), BF16),
            pltpu.VMEM((tokens, width), BF16),
            pltpu.VMEM((tokens + BLOCK, width), BF16),
            pltpu.VMEM((1, tokens), F32),
            pltpu.VMEM((1, width), F32),
            pltpu.SMEM(block_doc.shape, jnp.int32),
            pltpu.VMEM((3, hidden, width), BF16),
            pltpu.VMEM((3, rows, width), BF16),
            pltpu.VMEM((hidden, tokens), BF16),
            pltpu.VMEM((hidden, tokens), BF16),
            pltpu.VMEM((hidden, tokens), BF16),
            pltpu.VMEM((3, hidden, width), BF16),
            pltpu.VMEM((3, toks - 1, rows, width), BF16),
            pltpu.VMEM((3, rows, width), BF16),
            pltpu.VMEM((tokens, hidden), F32),
            pltpu.VMEM((tokens, hidden), BF16),
            pltpu.VMEM((tokens, width), F32),
            pltpu.VMEM((tokens, width), BF16),
            dma((10,)),
            dma((tiles,)),
            dma((2,)),
            dma((2,)),
            dma((3, toks - 1)),
            dma((3, toks - 1)),
            dma((3, toks)),
            dma((3, toks)),
        ],
        compiler_params=pltpu.CompilerParams(
            collective_id=0, has_side_effects=True, vmem_limit_bytes=48 << 20
        ),
    )(
        queries.reshape(tokens, width),
        keys.reshape(tokens, width),
        values.reshape(tokens, width),
        rates.reshape(1, tokens),
        w_in.reshape(w_in.shape[1:]),
        w_out.reshape(w_out.shape[1:]),
        gain,
        block_doc,
    )
    return out.reshape(queries.shape)


def solution(mesh):
    placed = (
        P(("groups", "span", "tok"), "head", None),
        P(("groups", "span", "tok"), "head", None),
        P(("groups", "span", "tok"), "head", None),
        P(("groups", "span", "tok"), "head"),
        P("head", None, None, None),
        P("head", None, None),
        P("head", None),
        P("groups"),
    )
    return jax.shard_map(
        functools.partial(body, mesh.shape["span"], mesh.shape["tok"]),
        mesh=mesh,
        in_specs=placed,
        out_specs=P(("groups", "span", "tok"), "head", None),
        check_vma=False,
    )
```

time: 98.9 us -> 34.5 us (0.35)
  the two profiles are of different devices: /device:TPU:0 before, /device:TPU:2 now
where the time goes in v1:
time: 34.5 us; the launch traced here: 34.2 us
  Pallas kernels  27.7 us (80%)
  local copies, waits for them, and re-layouts  6.46 us (19%)
    pallas_call x1, Pallas kernels, body(): pl.pallas_call(functools.partial(kernel, spans, toks), out_shape=jax.Shap...  27.7 us
    unnamed x17, local copies, waits for them, and re-layouts  6.46 us

profile of v1, /device:TPU:2, one launch (start us, length us, event | category | flops | bytes accessed | tf_op | source)
XLA Modules:
  0.0 34.2 jit_solution(1435533088221970203)
XLA Ops:
  0.0 0.0 copy-start.5
  0.0 0.0 copy-start.6
  0.0 0.0 copy-start.7
  0.0 0.7 %copy-done.5 = f32[1024,1]{0,1:T(1,128)S(1)} copy-done((f32[1024,1]{0,1:T(1,128)S(1)}, f32[1024,1]{0,1:T(1,128)}, u32[]{:S(2)}) %copy-start.5) | copy-done | bytes 4120
  0.7 0.0 copy-done.6
  0.7 0.0 copy-done.7
  0.7 0.0 copy-start
  0.7 1.0 %copy-done = bf16[1024,1,256]{2,0,1:T(8,128)(2,1)S(1)} copy-done((bf16[1024,1,256]{2,0,1:T(8,128)(2,1)S(1)}, bf16[1024,1,256]{2,0,1:T(8,128)(2,1)}, u32[]{:S(2)}) %copy-start) | copy-done | bytes 524312
  1.7 0.0 copy-start.1
  1.7 1.0 %copy-done.1 = bf16[1024,1,256]{2,0,1:T(8,128)(2,1)S(1)} copy-done((bf16[1024,1,256]{2,0,1:T(8,128)(2,1)S(1)}, bf16[1024,1,256]{2,0,1:T(8,128)(2,1)}, u32[]{:S(2)}) %copy-start.1) | copy-done | bytes 524312
  2.8 0.0 copy-start.2
  2.8 1.0 %copy-done.2 = bf16[1024,1,256]{2,0,1:T(8,128)(2,1)S(1)} copy-done((bf16[1024,1,256]{2,0,1:T(8,128)(2,1)S(1)}, bf16[1024,1,256]{2,0,1:T(8,128)(2,1)}, u32[]{:S(2)}) %copy-start.2) | copy-done | bytes 524312
  3.8 0.0 copy-start.3
  3.8 0.9 %copy-done.3 = bf16[1,2,256,256]{3,2,1,0:T(8,128)(2,1)S(1)} copy-done((bf16[1,2,256,256]{3,2,1,0:T(8,128)(2,1)S(1)}, bf16[1,2,256,256]{3,2,1,0:T(8,128)(2,1)}, u32[]{:S(2)}) %copy-start.3) | copy-done | bytes 262168
  4.8 0.0 copy-start.4
  4.8 0.9 %copy-done.4 = bf16[1,256,256]{2,1,0:T(8,128)(2,1)S(1)} copy-done((bf16[1,256,256]{2,1,0:T(8,128)(2,1)S(1)}, bf16[1,256,256]{2,1,0:T(8,128)(2,1)}, u32[]{:S(2)}) %copy-start.4) | copy-done | bytes 131096
  5.7 27.7 %shard_map.82 = bf16[1024,256]{1,0:T(8,128)(2,1)S(1)} custom-call(bf16[1024,256]{1,0:T(8,128)(2,1)S(1)} %bitcast.8, bf16[1024,256]{1,0:T(8,128)(2,1)S(1)} %bitcast.9, bf16[1024,256]{1,0:T(8,128)(2,1)S(1)} %bitcast.10, f32[1,1024]{1,0:T(1,128)S(1)} %bitcast.13, bf16[2,256,256]{2,1,0:T(8,128)(2,1)S(1)} %bitcast.11, bf16[256,256]{1,0:T(8,128)(2,1)S(1)} %bitcast.12, ...), custom_call_target="tpu_custom_call" | custom-call | tf_op jit(solution)/shard_map/pallas_call | solution.py:368
  33.4 0.8 %copy.10 = bf16[1024,1,256]{2,0,1:T(8,128)(2,1)} copy(bf16[1024,1,256]{2,0,1:T(8,128)(2,1)S(1)} %bitcast.7) | data formatting | bytes 1048576
Async XLA Ops:
  0.0 0.7 %copy-start.5 = (f32[1024,1]{0,1:T(1,128)S(1)}, f32[1024,1]{0,1:T(1,128)}, u32[]{:S(2)}) copy-start(f32[1024,1]{0,1:T(1,128)} %param.11) | copy-start | bytes 12292
  0.0 0.7 %copy-start.6 = (f32[1,256]{1,0:T(1,128)S(1)}, f32[1,256]{1,0:T(1,128)}, u32[]{:S(2)}) copy-start(f32[1,256]{1,0:T(1,128)} %gain_ref.1) | copy-start | bytes 3076
  0.0 0.7 %copy-start.7 = (s32[64]{0:T(128)S(1)}, s32[64]{0:T(128)}, u32[]{:S(2)}) copy-start(s32[64]{0:T(128)} %doc_ref.1) | copy-start | bytes 772
  0.7 1.0 %copy-start = (bf16[1024,1,256]{2,0,1:T(8,128)(2,1)S(1)}, bf16[1024,1,256]{2,0,1:T(8,128)(2,1)}, u32[]{:S(2)}) copy-start(bf16[1024,1,256]{2,0,1:T(8,128)(2,1)} %param.8) | copy-start | bytes 1572868
  1.7 1.0 %copy-start.1 = (bf16[1024,1,256]{2,0,1:T(8,128)(2,1)S(1)}, bf16[1024,1,256]{2,0,1:T(8,128)(2,1)}, u32[]{:S(2)}) copy-start(bf16[1024,1,256]{2,0,1:T(8,128)(2,1)} %param.9) | copy-start | bytes 1572868
  2.8 1.0 %copy-start.2 = (bf16[1024,1,256]{2,0,1:T(8,128)(2,1)S(1)}, bf16[1024,1,256]{2,0,1:T(8,128)(2,1)}, u32[]{:S(2)}) copy-start(bf16[1024,1,256]{2,0,1:T(8,128)(2,1)} %param.10) | copy-start | bytes 1572868
  3.8 0.9 %copy-start.3 = (bf16[1,2,256,256]{3,2,1,0:T(8,128)(2,1)S(1)}, bf16[1,2,256,256]{3,2,1,0:T(8,128)(2,1)}, u32[]{:S(2)}) copy-start(bf16[1,2,256,256]{3,2,1,0:T(8,128)(2,1)} %param.12) | copy-start | bytes 786436
  4.8 0.9 %copy-start.4 = (bf16[1,256,256]{2,1,0:T(8,128)(2,1)S(1)}, bf16[1,256,256]{2,1,0:T(8,128)(2,1)}, u32[]{:S(2)}) copy-start(bf16[1,256,256]{2,1,0:T(8,128)(2,1)} %param.13) | copy-start | bytes 393220

commit v2 on v1

--- a/solution.py
+++ b/solution.py
@@ -401,7 +401,7 @@
             dma((3, toks)),
         ],
         compiler_params=pltpu.CompilerParams(
-            collective_id=0, has_side_effects=True, vmem_limit_bytes=48 << 20
+            collective_id=0, has_side_effects=True, vmem_limit_bytes=60 << 20
         ),
     )(
         queries.reshape(tokens, width),

time: 34.5 us -> 29 us (0.84)
  local copies, waits for them, and re-layouts: 6.46 us -> 1.87 us
  Pallas kernels: 27.7 us -> 27 us
    unnamed x17 -> x1, local copies, waits for them, and re-layouts: 6.46 us -> 1.87 us
    pallas_call x1, Pallas kernels: 27.7 us -> 27 us  [body(): pl.pallas_call(functools.partial(kernel, spans, toks), out_shape=jax.Shap...]
where the time goes in v2:
time: 29 us; the launch traced here: 28.8 us
  Pallas kernels  27 us (93%)
  local copies, waits for them, and re-layouts  1.87 us (6%)
    pallas_call x1, Pallas kernels, body(): pl.pallas_call(functools.partial(kernel, spans, toks), out_shape=jax.Shap...  27 us
    unnamed x1, local copies, waits for them, and re-layouts  1.87 us

profile of v2, /device:TPU:2, one launch (start us, length us, event | category | flops | bytes accessed | tf_op | source)
XLA Modules:
  0.0 28.8 jit_solution(9110668964042723539)
XLA Ops:
  0.0 27.0 %shard_map.82 = bf16[1024,256]{1,0:T(8,128)(2,1)} custom-call(bf16[1024,256]{1,0:T(8,128)(2,1)} %bitcast.8, bf16[1024,256]{1,0:T(8,128)(2,1)} %bitcast.9, bf16[1024,256]{1,0:T(8,128)(2,1)} %bitcast.10, f32[1,1024]{1,0:T(1,128)} %bitcast.13, bf16[2,256,256]{2,1,0:T(8,128)(2,1)} %bitcast.11, bf16[256,256]{1,0:T(8,128)(2,1)} %bitcast.12, f32[1,256]{1,0:T(1,128)} %gain_ref.1, ...), custom_call_target="tpu_custom_call" | custom-call | tf_op jit(solution)/shard_map/pallas_call | solution.py:368
  27.0 1.9 %copy.10 = bf16[1024,1,256]{2,0,1:T(8,128)(2,1)} copy(bf16[1024,1,256]{2,0,1:T(8,128)(2,1)} %bitcast.7) | data formatting | bytes 1048576

commit v3 on v2

--- a/solution.py
+++ b/solution.py
@@ -71,6 +71,8 @@
     part_recv,
     fresh_send,
     fresh_recv,
+    spread_send,
+    spread_recv,
 ):
     tokens, width = q_ref.shape
     hidden = cur.shape[1]
@@ -170,13 +172,23 @@
             device_id_type=MESH,
         )
 
-    def fresh_copy(c, k):
+    def fresh_copy(c):
         return pltpu.make_async_remote_copy(
             fresh.at[c],
             cur.at[c, own],
-            fresh_send.at[c, k],
-            fresh_recv.at[c, k],
-            device_id=at(lax.rem(span + 1, spans), lax.rem(tok + k, toks)),
+            fresh_send.at[c],
+            fresh_recv.at[c],
+            device_id=at(lax.rem(span + 1, spans), tok),
+            device_id_type=MESH,
+        )
+
+    def spread_copy(c, k):
+        return pltpu.make_async_remote_copy(
+            cur.at[c, own],
+            cur.at[c, own],
+            spread_send.at[c, k - 1],
+            spread_recv.at[c, k - 1],
+            device_id=at(span, lax.rem(tok + k, toks)),
             device_id_type=MESH,
         )
 
@@ -223,15 +235,13 @@
             jnp.sum(updated * updated, axis=-1, keepdims=True) + EPSILON
         )
         fresh[c] = (updated * scale).astype(BF16)
-        for k in range(toks):
-            fresh_copy(c, k).start()
+        fresh_copy(c).start()
 
     def sent():
         for c in range(3):
             for k in range(1, toks):
                 part_copy(c, k).wait_send()
-            for k in range(toks):
-                fresh_copy(c, k).wait_send()
+            fresh_copy(c).wait_send()
 
     def norm_queries():
         q_load.wait()
@@ -300,8 +310,11 @@
             out_copy(i).start()
 
     def arrived(c):
-        for k in range(toks):
-            fresh_copy(c, k).wait_recv()
+        fresh_copy(c).wait_recv()
+        for k in range(1, toks):
+            spread_copy(c, k).start()
+        for k in range(1, toks):
+            spread_copy(c, k).wait_recv()
 
     @pl.when(span == 0)
     def _():
@@ -348,6 +361,9 @@
 
         else:
             apply_fast(arrived)
+        for c in range(3):
+            for k in range(1, toks):
+                spread_copy(c, k).wait_send()
 
     for i in range(tiles):
         out_copy(i).wait()
@@ -397,8 +413,10 @@
             dma((2,)),
             dma((3, toks - 1)),
             dma((3, toks - 1)),
-            dma((3, toks)),
-            dma((3, toks)),
+            dma((3,)),
+            dma((3,)),
+            dma((3, toks - 1)),
+            dma((3, toks - 1)),
         ],
         compiler_params=pltpu.CompilerParams(
             collective_id=0, has_side_effects=True, vmem_limit_bytes=60 << 20

time: 29 us -> 33.8 us (1.17)
  Pallas kernels: 27 us -> 31.8 us
    pallas_call x1, Pallas kernels: 27 us -> 31.8 us  [body(): pl.pallas_call(functools.partial(kernel, spans, toks), out_shape=jax.Shap...]
where the time goes in v3:
time: 33.8 us; the launch traced here: 33.6 us
  Pallas kernels  31.8 us (94%)
  local copies, waits for them, and re-layouts  1.87 us (6%)
    pallas_call x1, Pallas kernels, body(): pl.pallas_call(functools.partial(kernel, spans, toks), out_shape=jax.Shap...  31.8 us
    unnamed x1, local copies, waits for them, and re-layouts  1.87 us

profile of v3, /device:TPU:2, one launch (start us, length us, event | category | flops | bytes accessed | tf_op | source)
XLA Modules:
  0.0 33.6 jit_solution(7189478768498392153)
XLA Ops:
  0.0 31.8 %shard_map.82 = bf16[1024,256]{1,0:T(8,128)(2,1)} custom-call(bf16[1024,256]{1,0:T(8,128)(2,1)} %bitcast.8, bf16[1024,256]{1,0:T(8,128)(2,1)} %bitcast.9, bf16[1024,256]{1,0:T(8,128)(2,1)} %bitcast.10, f32[1,1024]{1,0:T(1,128)} %bitcast.13, bf16[2,256,256]{2,1,0:T(8,128)(2,1)} %bitcast.11, bf16[256,256]{1,0:T(8,128)(2,1)} %bitcast.12, f32[1,256]{1,0:T(1,128)} %gain_ref.1, ...), custom_call_target="tpu_custom_call" | custom-call | tf_op jit(solution)/shard_map/pallas_call | solution.py:384
  31.8 1.9 %copy.10 = bf16[1024,1,256]{2,0,1:T(8,128)(2,1)} copy(bf16[1024,1,256]{2,0,1:T(8,128)(2,1)} %bitcast.7) | data formatting | bytes 1048576

commit v4 on v2

--- a/solution.py
+++ b/solution.py
@@ -239,7 +239,7 @@
             piece = pl.ds(i * TILE, TILE)
             qn[piece] = rms_rows(q_raw[piece].astype(F32)).astype(BF16)
 
-    def attend():
+    def attend(between=None):
         doc_load.wait()
         row_pos = lax.broadcasted_iota(jnp.int32, (BLOCK, BLOCK), 0)
         col_pos = lax.broadcasted_iota(jnp.int32, (BLOCK, BLOCK), 1)
@@ -261,6 +261,8 @@
             attended[pl.ds(b * BLOCK, BLOCK)] = mixed / total
 
         for b in range(1, blocks):
+            if between is not None and b in (1, 3, 5):
+                between(b // 2)
             one(b)
 
         @pl.when(place > 0)
@@ -314,10 +316,7 @@
         start_out_load.wait()
         send_gradient()
         norm_queries()
-        attend()
-        pass_on(0)
-        pass_on(1)
-        pass_on(2)
+        attend(pass_on)
         apply_fast(lambda c: None)
         sent()
 

time: 29 us -> 29 us (level)
  no operation moved by 1% of the time
where the time goes in v4:
time: 29 us; the launch traced here: 28.8 us
  Pallas kernels  27 us (93%)
  local copies, waits for them, and re-layouts  1.87 us (6%)
    pallas_call x1, Pallas kernels, body(): pl.pallas_call(functools.partial(kernel, spans, toks), out_shape=jax.Shap...  27 us
    unnamed x1, local copies, waits for them, and re-layouts  1.87 us

profile of v4, /device:TPU:2, one launch (start us, length us, event | category | flops | bytes accessed | tf_op | source)
XLA Modules:
  0.0 28.8 jit_solution(3016241515073718464)
XLA Ops:
  0.0 27.0 %shard_map.82 = bf16[1024,256]{1,0:T(8,128)(2,1)} custom-call(bf16[1024,256]{1,0:T(8,128)(2,1)} %bitcast.8, bf16[1024,256]{1,0:T(8,128)(2,1)} %bitcast.9, bf16[1024,256]{1,0:T(8,128)(2,1)} %bitcast.10, f32[1,1024]{1,0:T(1,128)} %bitcast.13, bf16[2,256,256]{2,1,0:T(8,128)(2,1)} %bitcast.11, bf16[256,256]{1,0:T(8,128)(2,1)} %bitcast.12, f32[1,256]{1,0:T(1,128)} %gain_ref.1, ...), custom_call_target="tpu_custom_call" | custom-call | tf_op jit(solution)/shard_map/pallas_call | solution.py:367
  27.0 1.9 %copy.10 = bf16[1024,1,256]{2,0,1:T(8,128)(2,1)} copy(bf16[1024,1,256]{2,0,1:T(8,128)(2,1)} %bitcast.7) | data formatting | bytes 1048576

commit v5 on v3

--- a/solution.py
+++ b/solution.py
@@ -249,7 +249,7 @@
             piece = pl.ds(i * TILE, TILE)
             qn[piece] = rms_rows(q_raw[piece].astype(F32)).astype(BF16)
 
-    def attend():
+    def attend(between=None):
         doc_load.wait()
         row_pos = lax.broadcasted_iota(jnp.int32, (BLOCK, BLOCK), 0)
         col_pos = lax.broadcasted_iota(jnp.int32, (BLOCK, BLOCK), 1)
@@ -271,6 +271,8 @@
             attended[pl.ds(b * BLOCK, BLOCK)] = mixed / total
 
         for b in range(1, blocks):
+            if between is not None and b in (1, 3, 5):
+                between(b // 2)
             one(b)
 
         @pl.when(place > 0)
@@ -310,9 +312,11 @@
             out_copy(i).start()
 
     def arrived(c):
-        fresh_copy(c).wait_recv()
-        for k in range(1, toks):
-            spread_copy(c, k).start()
+        if c == 0:
+            for d in range(3):
+                fresh_copy(d).wait_recv()
+                for k in range(1, toks):
+                    spread_copy(d, k).start()
         for k in range(1, toks):
             spread_copy(c, k).wait_recv()
 
@@ -327,10 +331,7 @@
         start_out_load.wait()
         send_gradient()
         norm_queries()
-        attend()
-        pass_on(0)
-        pass_on(1)
-        pass_on(2)
+        attend(pass_on)
         apply_fast(lambda c: None)
         sent()
 

time: 33.8 us -> 27.8 us (0.82)
  Pallas kernels: 31.8 us -> 25.8 us
    pallas_call x1, Pallas kernels: 31.8 us -> 25.8 us  [body(): pl.pallas_call(functools.partial(kernel, spans, toks), out_shape=jax.Shap...]
where the time goes in v5:
time: 27.8 us; the launch traced here: 27.7 us
  Pallas kernels  25.8 us (93%)
  local copies, waits for them, and re-layouts  1.87 us (7%)
    pallas_call x1, Pallas kernels, body(): pl.pallas_call(functools.partial(kernel, spans, toks), out_shape=jax.Shap...  25.8 us
    unnamed x1, local copies, waits for them, and re-layouts  1.87 us

profile of v5, /device:TPU:2, one launch (start us, length us, event | category | flops | bytes accessed | tf_op | source)
XLA Modules:
  0.0 27.7 jit_solution(8018991938590840336)
XLA Ops:
  0.0 25.8 %shard_map.82 = bf16[1024,256]{1,0:T(8,128)(2,1)} custom-call(bf16[1024,256]{1,0:T(8,128)(2,1)} %bitcast.8, bf16[1024,256]{1,0:T(8,128)(2,1)} %bitcast.9, bf16[1024,256]{1,0:T(8,128)(2,1)} %bitcast.10, f32[1,1024]{1,0:T(1,128)} %bitcast.13, bf16[2,256,256]{2,1,0:T(8,128)(2,1)} %bitcast.11, bf16[256,256]{1,0:T(8,128)(2,1)} %bitcast.12, f32[1,256]{1,0:T(1,128)} %gain_ref.1, ...), custom_call_target="tpu_custom_call" | custom-call | tf_op jit(solution)/shard_map/pallas_call | solution.py:385
  25.8 1.9 %copy.10 = bf16[1024,1,256]{2,0,1:T(8,128)(2,1)} copy(bf16[1024,1,256]{2,0,1:T(8,128)(2,1)} %bitcast.7) | data formatting | bytes 1048576
